TPU v7x, 512 devices: a whole 4x8x8 slice. The times are simulated.
512 devices in a mesh: row: 32 (over z_lo, y, core), col: 16 (over x, z_hi).
Axes of the slice: x: 4, y: 8, z: 8 (z_hi: 4, z_lo: 2; z = z_hi * 2 + z_lo), core: 2. Of those that a mesh axis runs over, the one named last changes fastest.
Arguments:
- amplitudes: bfloat16 [512, 160, 256], P(('row', 'col')), may hold values from -6 to 6
- tile_edges: int32 [512], P(('row', 'col')), may hold values from 96 to 160
- integrals: bfloat16 [512, 16, 5, 160, 160], P('row', 'col'), may hold values from -0.078125 to 0.078125
- source_rows: int32 [512, 16, 5], P('row', 'col'), may hold values from 0 to 31, as said below
- live_counts: int32 [512, 16], P('row', 'col'), may hold values from 2 to 5
Outputs:
- residual: float32 [512, 160, 256], P(('row', 'col'))
Inputs may be any that keep to these rules, and one draw needn't show every extreme that they name: source_rows[a, c, j] differs from a // 16 by at most 3.
All inputs are finite; a program needn't handle non-finite values.
Results may differ from a plain program's by a relative error of at most 0.0003.
Values may be sent and summed in bfloat16 or wider, within the bound.
A program may use at most 64 MiB of HBM per device.

v0:
```python
import jax
import jax.numpy as jnp
from jax import lax
from jax.sharding import PartitionSpec as P

HALF = 3


def passed_along(value, axis, by):
    size = lax.axis_size(axis)
    pairs = [(i, i + by) for i in range(size) if 0 <= i + by < size]
    return lax.ppermute(value, axis, pairs)


def per_device(amplitudes, tile_edges, integrals, source_rows, live_counts):
    size_edge = amplitudes.shape[1]
    positions = jnp.arange(size_edge)
    masked = jnp.where(
        positions[None, :, None] < tile_edges[:, None, None], amplitudes, jnp.zeros_like(amplitudes)
    )
    my_row = lax.axis_index("row")
    pieces = []
    for offset in range(-HALF, HALF + 1):
        if offset == 0:
            pieces.append(masked)
        else:
            pieces.append(passed_along(masked, "row", -offset))
    window = jnp.concatenate(pieces, axis=0)
    lowest = my_row - HALF
    slots = jnp.arange(integrals.shape[2])
    weights = integrals[:, 0]
    rows_from = source_rows[:, 0]
    alive_count = live_counts[:, 0]
    places = rows_from - lowest
    picked = jnp.take(window, places, axis=0)
    alive = slots[None, :] < alive_count[:, None]
    picked = jnp.where(alive[:, :, None, None], picked, jnp.zeros_like(picked))
    share = lax.psum_scatter(
        jnp.einsum("abxy,abyp->axp", weights, picked, preferred_element_type=jnp.float32),
        "col",
        scatter_dimension=0,
        tiled=True,
    )
    return jnp.where(
        positions[None, :, None] < tile_edges[:, None, None], share, jnp.zeros_like(share)
    )


def solution(mesh):
    return jax.shard_map(
        per_device,
        mesh=mesh,
        in_specs=(
            P(("row", "col"), None, None),
            P(("row", "col")),
            P("row", "col", None, None, None),
            P("row", "col", None),
            P("row", "col"),
        ),
        out_specs=P(("row", "col"), None, None),
        check_vma=False,
    )
```

profile of v0, /device:TPU:32, one launch (start us, length us, event | category | flops | bytes accessed | tf_op | source)
XLA Modules:
  0.0 159.7 jit_solution(15318669150203520520)
XLA Ops:
  6.5 0.0 reduce-scatter.2.cloned.1.call-start
  7.2 1.0 broadcast_select_fusion.1
  8.2 1.9 %collective-permute-start.5 = (bf16[1,160,256]{2,1,0:T(8,128)(2,1)S(1)}, bf16[1,160,256]{2,1,0:T(8,128)(2,1)S(1)}, u32[]{:S(2)}, u32[]{:S(2)}) collective-permute-start(bf16[1,160,256]{2,1,0:T(8,128)(2,1)S(1)} %broadcast_select_fusion.1), channel_id=1, source_target_pairs={{48,0},{64,16},{80,32},{96,48},{112,64},{128,80},{144,96},{160,112... | collective-permute-start | bytes 245768 | tf_op jit(solution)/shard_map/ppermute | solution.py:12
  10.1 2.4 %collective-permute-start.4 = (bf16[1,160,256]{2,1,0:T(8,128)(2,1)S(1)}, bf16[1,160,256]{2,1,0:T(8,128)(2,1)S(1)}, u32[]{:S(2)}, u32[]{:S(2)}) collective-permute-start(bf16[1,160,256]{2,1,0:T(8,128)(2,1)S(1)} %broadcast_select_fusion.1), channel_id=1, source_target_pairs={{32,0},{48,16},{64,32},{80,48},{96,64},{112,80},{128,96},{144,112}... | collective-permute-start | bytes 245768 | tf_op jit(solution)/shard_map/ppermute | solution.py:12
  12.5 2.2 %collective-permute-start.3 = (bf16[1,160,256]{2,1,0:T(8,128)(2,1)S(1)}, bf16[1,160,256]{2,1,0:T(8,128)(2,1)S(1)}, u32[]{:S(2)}, u32[]{:S(2)}) collective-permute-start(bf16[1,160,256]{2,1,0:T(8,128)(2,1)S(1)} %broadcast_select_fusion.1), channel_id=1, source_target_pairs={{16,0},{32,16},{48,32},{64,48},{80,64},{96,80},{112,96},{128,112},... | collective-permute-start | bytes 245768 | tf_op jit(solution)/shard_map/ppermute | solution.py:12
  14.7 2.1 %collective-permute-start.2 = (bf16[1,160,256]{2,1,0:T(8,128)(2,1)S(1)}, bf16[1,160,256]{2,1,0:T(8,128)(2,1)S(1)}, u32[]{:S(2)}, u32[]{:S(2)}) collective-permute-start(bf16[1,160,256]{2,1,0:T(8,128)(2,1)S(1)} %broadcast_select_fusion.1), channel_id=1, source_target_pairs={{0,16},{16,32},{32,48},{48,64},{64,80},{80,96},{96,112},{112,128},... | collective-permute-start | bytes 245768 | tf_op jit(solution)/shard_map/ppermute | solution.py:12
  16.8 4.6 %collective-permute-start = (bf16[1,160,256]{2,1,0:T(8,128)(2,1)S(1)}, bf16[1,160,256]{2,1,0:T(8,128)(2,1)S(1)}, u32[]{:S(2)}, u32[]{:S(2)}) collective-permute-start(bf16[1,160,256]{2,1,0:T(8,128)(2,1)S(1)} %broadcast_select_fusion.1), channel_id=1, source_target_pairs={{0,48},{16,64},{32,80},{48,96},{64,112},{80,128},{96,144},{112,160... | collective-permute-start | bytes 245768 | tf_op jit(solution)/shard_map/ppermute | solution.py:12
  21.4 0.7 compare_and_fusion
  22.1 0.7 copy_subtract_fusion
  22.8 0.1 copy.10
  22.9 0.7 iota_compare_fusion
  23.6 0.1 copy.11
  23.7 0.1 reshape.63
  23.8 3.8 %collective-permute-done = bf16[1,160,256]{2,1,0:T(8,128)(2,1)S(1)} collective-permute-done((bf16[1,160,256]{2,1,0:T(8,128)(2,1)S(1)}, bf16[1,160,256]{2,1,0:T(8,128)(2,1)S(1)}, u32[]{:S(2)}, u32[]{:S(2)}) %collective-permute-start) | collective-permute-done | bytes 81952 | tf_op jit(solution)/shard_map/ppermute | solution.py:12
  27.7 1.9 %collective-permute-start.1 = (bf16[1,160,256]{2,1,0:T(8,128)(2,1)S(1)}, bf16[1,160,256]{2,1,0:T(8,128)(2,1)S(1)}, u32[]{:S(2)}, u32[]{:S(2)}) collective-permute-start(bf16[1,160,256]{2,1,0:T(8,128)(2,1)S(1)} %broadcast_select_fusion.1), channel_id=1, source_target_pairs={{0,32},{16,48},{32,64},{48,80},{64,96},{80,112},{96,128},{112,144}... | collective-permute-start | bytes 245768 | tf_op jit(solution)/shard_map/ppermute | solution.py:12
  29.6 5.6 %collective-permute-done.1 = bf16[1,160,256]{2,1,0:T(8,128)(2,1)S(1)} collective-permute-done((bf16[1,160,256]{2,1,0:T(8,128)(2,1)S(1)}, bf16[1,160,256]{2,1,0:T(8,128)(2,1)S(1)}, u32[]{:S(2)}, u32[]{:S(2)}) %collective-permute-start.1) | collective-permute-done | bytes 81952 | tf_op jit(solution)/shard_map/ppermute | solution.py:12
  35.2 0.0 collective-permute-done.2
  35.2 1.0 constant_dynamic-update-slice_fusion.3
  36.2 0.0 collective-permute-done.3
  36.2 0.0 collective-permute-done.4
  36.3 0.0 collective-permute-done.5
  36.3 6.3 %gather_fusion = bf16[80,160,256]{2,1,0:T(8,128)(2,1)} fusion(bf16[7,160,256]{2,1,0:T(8,128)(2,1)S(1)} %constant_dynamic-update-slice_fusion, s32[1024]{0:T(1024)S(1)} %pad_clamp_fusion), kind=kCustom, calls=%fused_computation | custom fusion | bytes 13107520 | tf_op jit(solution)/shard_map/jit(_take)/gather | solution.py:35
  42.6 8.3 %fusion.8 = f32[16,160,256]{2,1,0:T(8,128)} fusion(bf16[16,5,160,256]{3,2,1,0:T(8,128)(2,1)} %bitcast.21, pred[16,5]{1,0:T(8,128)(4,1)S(1)} %copy.10, pred[16,5]{1,0:T(8,128)(4,1)S(1)} %iota_compare_fusion, bf16[16,1,5,160,160]{4,3,2,1,0:T(8,128)(2,1)} %param.7), kind=kOutput, calls=%fused_computation.9 | convolution fusion | flops 1055129600 | bytes 13271200 | tf_op jit(solution)/shard_map/abxy,abyp->axp/dot_general | solution.py:39
  50.9 0.0 reduce-scatter.2.cloned.1.call-update
  50.9 100.3 %reduce-scatter.2.cloned.1.call-done = f32[1,160,256]{2,1,0:T(8,128)} async-done(((f32[16,160,256]{2,1,0:T(8,128)}), f32[1,160,256]{2,1,0:T(8,128)}) %reduce-scatter.2.cloned.1.call-update) | async-done | bytes 163856 | tf_op jit(solution)/shard_map/reduce_scatter | solution.py:38
  151.2 1.7 %broadcast_select_fusion = f32[1,160,256]{2,1,0:T(8,128)} fusion(f32[1,160,256]{2,1,0:T(8,128)} %reduce-scatter.2.cloned.1.call-done, pred[160]{0:T(512)(128)(4,1)S(1)} %iota_compare_fusion.1), kind=kLoop, calls=%fused_computation.10 | loop fusion | flops 40960 | bytes 327840 | tf_op jit(solution)/shard_map/jit(_where)/select_n | solution.py:44
  (9 shorter events, 0.1 us)
Async XLA Ops:
  6.5 144.7 %reduce-scatter.2.cloned.1.call-start = ((), (), s32[]{:S(2)}) async-start(), calls=%async_computation.1 | async-start | bytes 2785280 | tf_op jit(solution)/shard_map/reduce_scatter | solution.py:38
  8.2 28.1 %collective-permute-start.5 = (bf16[1,160,256]{2,1,0:T(8,128)(2,1)S(1)}, bf16[1,160,256]{2,1,0:T(8,128)(2,1)S(1)}, u32[]{:S(2)}, u32[]{:S(2)}) collective-permute-start(bf16[1,160,256]{2,1,0:T(8,128)(2,1)S(1)} %broadcast_select_fusion.1), channel_id=1, source_target_pairs={{48,0},{64,16},{80,32},{96,48},{112,64},{128,80},{144,96},{160,112... | collective-permute-start | bytes 245768 | tf_op jit(solution)/shard_map/ppermute | solution.py:12
  10.1 26.1 %collective-permute-start.4 = (bf16[1,160,256]{2,1,0:T(8,128)(2,1)S(1)}, bf16[1,160,256]{2,1,0:T(8,128)(2,1)S(1)}, u32[]{:S(2)}, u32[]{:S(2)}) collective-permute-start(bf16[1,160,256]{2,1,0:T(8,128)(2,1)S(1)} %broadcast_select_fusion.1), channel_id=1, source_target_pairs={{32,0},{48,16},{64,32},{80,48},{96,64},{112,80},{128,96},{144,112}... | collective-permute-start | bytes 245768 | tf_op jit(solution)/shard_map/ppermute | solution.py:12
  12.5 23.7 %collective-permute-start.3 = (bf16[1,160,256]{2,1,0:T(8,128)(2,1)S(1)}, bf16[1,160,256]{2,1,0:T(8,128)(2,1)S(1)}, u32[]{:S(2)}, u32[]{:S(2)}) collective-permute-start(bf16[1,160,256]{2,1,0:T(8,128)(2,1)S(1)} %broadcast_select_fusion.1), channel_id=1, source_target_pairs={{16,0},{32,16},{48,32},{64,48},{80,64},{96,80},{112,96},{128,112},... | collective-permute-start | bytes 245768 | tf_op jit(solution)/shard_map/ppermute | solution.py:12
  14.7 20.5 %collective-permute-start.2 = (bf16[1,160,256]{2,1,0:T(8,128)(2,1)S(1)}, bf16[1,160,256]{2,1,0:T(8,128)(2,1)S(1)}, u32[]{:S(2)}, u32[]{:S(2)}) collective-permute-start(bf16[1,160,256]{2,1,0:T(8,128)(2,1)S(1)} %broadcast_select_fusion.1), channel_id=1, source_target_pairs={{0,16},{16,32},{32,48},{48,64},{64,80},{80,96},{96,112},{112,128},... | collective-permute-start | bytes 245768 | tf_op jit(solution)/shard_map/ppermute | solution.py:12
  16.8 10.9 %collective-permute-start = (bf16[1,160,256]{2,1,0:T(8,128)(2,1)S(1)}, bf16[1,160,256]{2,1,0:T(8,128)(2,1)S(1)}, u32[]{:S(2)}, u32[]{:S(2)}) collective-permute-start(bf16[1,160,256]{2,1,0:T(8,128)(2,1)S(1)} %broadcast_select_fusion.1), channel_id=1, source_target_pairs={{0,48},{16,64},{32,80},{48,96},{64,112},{80,128},{96,144},{112,160... | collective-permute-start | bytes 245768 | tf_op jit(solution)/shard_map/ppermute | solution.py:12
  27.7 7.5 %collective-permute-start.1 = (bf16[1,160,256]{2,1,0:T(8,128)(2,1)S(1)}, bf16[1,160,256]{2,1,0:T(8,128)(2,1)S(1)}, u32[]{:S(2)}, u32[]{:S(2)}) collective-permute-start(bf16[1,160,256]{2,1,0:T(8,128)(2,1)S(1)} %broadcast_select_fusion.1), channel_id=1, source_target_pairs={{0,32},{16,48},{32,64},{48,80},{64,96},{80,112},{96,128},{112,144}... | collective-permute-start | bytes 245768 | tf_op jit(solution)/shard_map/ppermute | solution.py:12
Sparse Core Ops, SparseCore 0:
  51.0 100.1 reduce-scatter.1
where the time goes:
time: 160 us
  waiting for transfers between devices  110 us (69%)
  starting transfers between devices  15.1 us (9%)
  between operations  14.2 us (9%)
  matrix products  8.26 us (5%)
  local copies, waits for them, and re-layouts  6.64 us (4%)
  other arithmetic  5.75 us (4%)
    reduce_scatter x1, waiting for transfers between devices, per_device(): lax.psum_scatter(jnp.einsum('abxy,abyp->axp', weights, picked, preferred_...  100 us
    ppermute x6, starting transfers between devices, passed_along(): return lax.ppermute(value, axis, pairs)  15.1 us
    ppermute x6, waiting for transfers between devices, passed_along(): return lax.ppermute(value, axis, pairs)  9.45 us
    dot_general x1, matrix products, per_device(): jnp.einsum('abxy,abyp->axp', weights, picked, preferred_element_type=jnp....  8.26 us
    gather x1, local copies, waits for them, and re-layouts, per_device(): picked = jnp.take(window, places, axis=0)  6.33 us
  transfers between devices with their start and end apart: 7, of which 3 were waited for; matrix products, arithmetic and copies ran while one was open for 2% of the time, Pallas kernels for 0%

commit v1 on v0

v1 whole, which is shorter than its diff:
```python
import functools

import jax
import jax.numpy as jnp
from jax import lax
from jax.experimental import pallas as pl
from jax.experimental.pallas import tpu as pltpu
from jax.sharding import PartitionSpec as P

HALF = 3
SIDE = 4
DEAD = 2 * HALF + 1
EXP_ROWS = 16
TINY = 2.0**-110
LANES = 128

WAY = {
    (0, 2, 0): "up",
    (0, 2, 1): "down",
    (2, 0, 0): "left",
    (2, 0, 1): "right",
    (2, 1, 0): "up",
    (2, 1, 1): "up",
    (2, 2, 0): "left",
    (2, 2, 1): "right_2",
    (2, 3, 0): "down",
    (2, 3, 1): "down",
}

SEND, PASS, ALL = 3, 4, 5
ORDER = (
    (1, 1, 0), (1, 1, 0, SEND), (2, 2, 0), (2, 2, 0, SEND), (1, 2, 0), (PASS,), (1, 2, 0, SEND), (0, 0, 0),
    (2, 3, 0), (2, 3, 0, SEND), (0, 2, 0), (ALL,), (2, 2, 1), (2, 2, 1, SEND), (3, 2, 2), (3, 2, 1, SEND),
    (2, 1, 2), (2, 1, 1, SEND), (3, 3, 2), (1, 2, 1), (1, 2, 1, SEND), (3, 2, 0, SEND), (2, 1, 0, SEND),
    (3, 3, 0, SEND), (2, 3, 1), (2, 3, 1, SEND), (1, 1, 1), (1, 1, 1, SEND), (1, 3, 2), (1, 3, 0, SEND),
    (3, 1, 2), (3, 1, 1, SEND), (3, 1, 0, SEND), (0, 1, 2), (0, 2, 1), (0, 0, 1), (3, 3, 1, SEND), (2, 0, 2),
    (0, 2, 0, SEND), (0, 2, 1, SEND), (1, 0, 2), (1, 3, 1, SEND), (3, 0, 2), (3, 0, 1, SEND), (0, 3, 2),
    (1, 0, 0, SEND), (2, 0, 1, SEND), (0, 1, 1, SEND), (0, 3, 0, SEND), (2, 0, 0, SEND), (0, 1, 0, SEND),
    (0, 3, 1, SEND), (3, 0, 0, SEND), (1, 0, 1, SEND),
)


MOVES = {"right": (1, 0), "left": (-1, 0), "up": (0, 1), "down": (0, -1), "right_2": (2, 0), "up_2": (0, 2)}


def way(dx, dz, side):
    if (dx, dz, side) in WAY:
        return WAY[dx, dz, side]
    if dx:
        return "right" if dx == 1 else "left"
    return "up" if dz == 1 else "down"


def onward(dx, dz, side):
    by_x, by_z = MOVES[way(dx, dz, side)]
    return (dx - by_x) % SIDE, (dz - by_z) % SIDE, side


NODES = [(dx, dz, side) for dx in range(SIDE) for dz in range(SIDE) for side in (0, 1) if dx or dz]


def arriving(node):
    return [other for other in NODES if onward(*other) == node]


def kernel(
    size, rows,
    amp_ref, edge_ref, src_ref, live_ref, weight_ref, out_ref,
    amp, src, live, weight, window_0, window_1, part, outbox, inbox,
    load_sem, row_send, row_recv, send_sem, recv_sem,
):
    window = (window_0, window_1)
    slots = weight_ref.shape[2]
    edge_len = amp_ref.shape[1]
    me_row = lax.axis_index("row")
    me_col = lax.axis_index("col")
    me_x = me_col // SIDE
    me_z = me_col % SIDE

    def row_at(by):
        return {"row": lax.rem(me_row + by + rows, rows)}

    def col_at(by_x, by_z):
        return {"col": lax.rem(me_x + by_x + SIDE, SIDE) * SIDE + lax.rem(me_z + by_z + SIDE, SIDE)}

    used = {way(*node) for node in NODES}
    neighbours = {name: col_at(*by) for name, by in MOVES.items() if name in used}

    amp_copy = pltpu.make_async_copy(amp_ref.at[0], amp, load_sem.at[0])
    amp_copy.start()
    barrier = pltpu.get_barrier_semaphore()
    core = lax.rem(me_row, 2)
    beyond = 6 * core - HALF
    sibling = 1 - 2 * core
    chip, last_chip = me_row // 2, rows // 2 - 1
    has = {2: chip < last_chip, -2: chip > 0}
    has_beyond = jnp.logical_and(me_row + beyond >= 0, me_row + beyond < rows)

    def where(condition, act):
        if condition is None:
            act()
        else:
            pl.when(condition)(act)

    def greet(partner):
        pl.semaphore_signal(barrier, inc=1, device_id=partner, device_id_type=pl.DeviceIdType.MESH)

    for partner in [row_at(sibling), *neighbours.values()]:
        greet(partner)
    row_partners = [(2, has[2]), (-2, has[-2]), (beyond, has_beyond)]
    for by, condition in row_partners:
        where(condition, functools.partial(greet, row_at(by)))
    expected = 1 + len(neighbours) + sum(condition.astype(jnp.int32) for _, condition in row_partners)
    loads = [
        pltpu.make_async_copy(src_ref, src, load_sem.at[1]),
        pltpu.make_async_copy(live_ref, live, load_sem.at[2]),
        pltpu.make_async_copy(weight_ref.at[:, 0], weight, load_sem.at[3]),
    ]
    edge = edge_ref[0]
    kept = lax.broadcasted_iota(jnp.int32, (edge_len, LANES), 0) < edge
    for side in (0, 1):
        window[side][DEAD] = jnp.zeros((edge_len, LANES), amp.dtype)
    amp_copy.wait()
    for side in (0, 1):
        columns = amp[:, side * LANES:(side + 1) * LANES].astype(jnp.float32)
        window[side][HALF] = jnp.where(kept, columns, 0.0).astype(amp.dtype)
    pl.semaphore_wait(barrier, expected)

    def row_copy(side, place, source, target, by):
        return pltpu.make_async_remote_copy(
            src_ref=window[side].at[source],
            dst_ref=window[side].at[target],
            send_sem=row_send.at[6 * side + place],
            recv_sem=row_recv.at[6 * side + place],
            device_id=row_at(by),
            device_id_type=pl.DeviceIdType.MESH,
        )

    own = [
        [
            (row_copy(side, 0, HALF, HALF - 2, 2), has[2], has[-2]),
            (row_copy(side, 1, HALF, HALF + 2, -2), has[-2], has[2]),
            (row_copy(side, 2, HALF, HALF - sibling, sibling), None, None),
            (row_copy(side, 3, HALF, HALF - beyond, beyond), has_beyond, has_beyond),
        ]
        for side in (0, 1)
    ]
    passed_on = [
        [
            (row_copy(side, 4, HALF - 2, HALF - 2 - sibling, sibling), has[-2], has[-2]),
            (row_copy(side, 5, HALF + 2, HALF + 2 - sibling, sibling), has[2], has[2]),
        ]
        for side in (0, 1)
    ]
    for copy, sends, _ in own[0] + own[1]:
        where(sends, copy.start)
    for copy in loads:
        copy.start()

    def pass_on(side):
        for (arrived, _, receives), (copy, _, _) in zip(own[side], passed_on[side]):
            def forward(arrived=arrived, copy=copy):
                arrived.wait_recv()
                copy.start()

            where(receives, forward)

    def wait_window(side):
        for copy, _, receives in own[side][2:] + passed_on[side]:
            where(receives, copy.wait_recv)

    def place_of(node):
        return (node[0] * SIDE + node[1] - 1) * 2 + node[2]

    def message(node):
        place = place_of(node)
        return pltpu.make_async_remote_copy(
            src_ref=outbox.at[place],
            dst_ref=inbox.at[place],
            send_sem=send_sem.at[place],
            recv_sem=recv_sem.at[place],
            device_id=neighbours[way(*node)],
            device_id_type=pl.DeviceIdType.MESH,
        )

    messages = {node: message(node) for node in NODES}

    def multiply(dx, dz, sides):
        tile = lax.rem(me_x + dx, SIDE) * SIDE + lax.rem(me_z + dz, SIDE)
        count = live[0, tile]
        total = None
        for slot in range(slots):
            place = jnp.where(slot < count, src[slot, 0, tile] - me_row + HALF, DEAD)
            columns = [window[side][place] for side in sides]
            columns = columns[0] if len(columns) == 1 else jnp.concatenate(columns, axis=1)
            term = jnp.dot(weight[tile, slot], columns, preferred_element_type=jnp.float32)
            total = term if total is None else total + term
        for place, side in enumerate(sides):
            part[side, dx * SIDE + dz] = total[:, place * LANES:(place + 1) * LANES]

    def summed(node):
        value = part[node[2], node[0] * SIDE + node[1]]
        for other in arriving(node):
            messages[other].wait_recv()
            place = place_of(other)
            exponent = inbox[place, edge_len:].astype(jnp.float32)[:1]
            value += inbox[place, :edge_len].astype(jnp.float32) * jnp.exp2(exponent)
        return value

    def send(node):
        value = summed(node)
        place = place_of(node)
        most = jnp.maximum(jnp.max(jnp.abs(value), axis=0, keepdims=True), TINY)
        exponent = jnp.ceil(jnp.log2(most * 1.0001)) - 15.0
        outbox[place, :edge_len] = jnp.round(value * jnp.exp2(-exponent)).astype(jnp.int16)
        outbox[place, edge_len:] = jnp.broadcast_to(exponent, (EXP_ROWS, LANES)).astype(jnp.int16)
        messages[node].start()

    pass_on(0)
    for copy in loads:
        copy.wait()
    wait_window(0)
    for step in ORDER:
        kind = step[-1]
        if kind == SEND:
            send(step[:3])
        elif kind == PASS:
            pass_on(1)
        elif kind == ALL:
            wait_window(1)
        else:
            multiply(*step[:2], (0, 1) if kind == 2 else (kind,))

    for side in (0, 1):
        out_ref[0, :, side * LANES:(side + 1) * LANES] = jnp.where(kept, summed((0, 0, side)), 0.0)
    for copy, sends, _ in own[0] + own[1] + passed_on[0] + passed_on[1]:
        where(sends, copy.wait_send)
    for copy in messages.values():
        copy.wait_send()


def per_device(rows, amplitudes, tile_edges, integrals, source_rows, live_counts):
    size, _, slots, edge_len, _ = integrals.shape
    width = amplitudes.shape[2]
    any_space = pl.BlockSpec(memory_space=pl.ANY)
    in_hbm = functools.partial(pltpu.with_memory_space_constraint, memory_space=pltpu.HBM)
    return pl.pallas_call(
        functools.partial(kernel, size, rows),
        out_shape=pltpu.VMEM((1, edge_len, width), jnp.float32),
        in_specs=[any_space, pl.BlockSpec(memory_space=pltpu.SMEM), any_space, any_space, any_space],
        out_specs=pl.BlockSpec(memory_space=pltpu.VMEM),
        scratch_shapes=[
            pltpu.VMEM((edge_len, width), amplitudes.dtype),
            pltpu.SMEM((slots, 1, size), jnp.int32),
            pltpu.SMEM((1, size), jnp.int32),
            pltpu.VMEM((size, slots, edge_len, edge_len), integrals.dtype),
            pltpu.VMEM((2 * HALF + 2, edge_len, LANES), amplitudes.dtype),
            pltpu.VMEM((2 * HALF + 2, edge_len, LANES), amplitudes.dtype),
            pltpu.VMEM((2, size, edge_len, LANES), jnp.float32),
            pltpu.VMEM((len(NODES), edge_len + EXP_ROWS, LANES), jnp.int16),
            pltpu.VMEM((len(NODES), edge_len + EXP_ROWS, LANES), jnp.int16),
            pltpu.SemaphoreType.DMA((4,)),
            pltpu.SemaphoreType.DMA((12,)),
            pltpu.SemaphoreType.DMA((12,)),
            pltpu.SemaphoreType.DMA((len(NODES),)),
            pltpu.SemaphoreType.DMA((len(NODES),)),
        ],
        compiler_params=pltpu.CompilerParams(
            collective_id=0, has_side_effects=True, vmem_limit_bytes=60 * 1024 * 1024
        ),
        cost_estimate=pl.CostEstimate(
            flops=2 * size * slots * edge_len * edge_len * width,
            bytes_accessed=2 * size * slots * edge_len * edge_len,
            transcendentals=0,
        ),
    )(
        in_hbm(amplitudes),
        tile_edges,
        in_hbm(source_rows.transpose(2, 1, 0)),
        in_hbm(live_counts.transpose(1, 0)),
        in_hbm(integrals),
    )


def solution(mesh):
    return jax.shard_map(
        functools.partial(per_device, mesh.shape["row"]),
        mesh=mesh,
        in_specs=(
            P(("row", "col"), None, None),
            P(("row", "col")),
            P("row", "col", None, None, None),
            P("row", "col", None),
            P("row", "col"),
        ),
        out_specs=P(("row", "col"), None, None),
        check_vma=False,
    )
```

time: 160 us -> 37.2 us (0.23)
  the two profiles are of different devices: /device:TPU:32 before, /device:TPU:16 now
where the time goes in v1:
time: 37.2 us; the launch traced here: 37.1 us
  Pallas kernels  35.8 us (96%)
  local copies, waits for them, and re-layouts  0.67 us (2%)
  between operations  0.66 us (2%)
    pallas_call x1, Pallas kernels, per_device(): pl.pallas_call(functools.partial(kernel, size, rows), out_shape=pltpu.VME...  35.8 us

profile of v1, /device:TPU:16, one launch (start us, length us, event | category | flops | bytes accessed | tf_op | source)
XLA Modules:
  0.0 37.1 jit_solution(9266724604502816358)
XLA Ops:
  0.7 35.8 %shard_map.55 = f32[1,160,256]{2,1,0:T(8,128)S(1)} custom-call(bf16[1,160,256]{2,1,0:T(8,128)(2,1)} %amp_ref.1, s32[1]{0:T(128)S(6)} %copy.8.edge_ref, s32[5,1,16]{2,1,0:T(1,128)} %bitcast.2, s32[1,16]{1,0:T(1,128)} %bitcast.3, bf16[16,1,5,160,160]{4,3,2,1,0:T(8,128)(2,1)} %weight_ref.1), custom_call_target="tpu_custom_call" | custom-call | flops 1048576000 | bytes 4096000 | tf_op jit(solution)/shard_map/pallas_call | solution.py:247
  36.4 0.7 %copy.7 = f32[1,160,256]{2,1,0:T(8,128)} copy(f32[1,160,256]{2,1,0:T(8,128)S(1)} %shard_map.55) | data formatting | bytes 327680

commit v2 on v1

--- a/solution.py
+++ b/solution.py
@@ -16,7 +16,7 @@
 
 WAY = {
     (0, 2, 0): "up",
-    (0, 2, 1): "down",
+    (0, 2, 1): "up_2",
     (2, 0, 0): "left",
     (2, 0, 1): "right",
     (2, 1, 0): "up",
@@ -29,14 +29,14 @@
 
 SEND, PASS, ALL = 3, 4, 5
 ORDER = (
-    (1, 1, 0), (1, 1, 0, SEND), (2, 2, 0), (2, 2, 0, SEND), (1, 2, 0), (PASS,), (1, 2, 0, SEND), (0, 0, 0),
-    (2, 3, 0), (2, 3, 0, SEND), (0, 2, 0), (ALL,), (2, 2, 1), (2, 2, 1, SEND), (3, 2, 2), (3, 2, 1, SEND),
-    (2, 1, 2), (2, 1, 1, SEND), (3, 3, 2), (1, 2, 1), (1, 2, 1, SEND), (3, 2, 0, SEND), (2, 1, 0, SEND),
-    (3, 3, 0, SEND), (2, 3, 1), (2, 3, 1, SEND), (1, 1, 1), (1, 1, 1, SEND), (1, 3, 2), (1, 3, 0, SEND),
-    (3, 1, 2), (3, 1, 1, SEND), (3, 1, 0, SEND), (0, 1, 2), (0, 2, 1), (0, 0, 1), (3, 3, 1, SEND), (2, 0, 2),
-    (0, 2, 0, SEND), (0, 2, 1, SEND), (1, 0, 2), (1, 3, 1, SEND), (3, 0, 2), (3, 0, 1, SEND), (0, 3, 2),
-    (1, 0, 0, SEND), (2, 0, 1, SEND), (0, 1, 1, SEND), (0, 3, 0, SEND), (2, 0, 0, SEND), (0, 1, 0, SEND),
-    (0, 3, 1, SEND), (3, 0, 0, SEND), (1, 0, 1, SEND),
+    (2, 2, 0), (2, 2, 0, SEND), (1, 2, 0), (1, 2, 0, SEND), (PASS,), (2, 3, 0), (2, 3, 0, SEND), (1, 3, 0),
+    (1, 3, 0, SEND), (3, 3, 0), (3, 3, 0, SEND), (ALL,), (2, 2, 1), (2, 2, 1, SEND), (2, 3, 1), (2, 1, 2),
+    (2, 1, 1, SEND), (3, 2, 2), (2, 3, 1, SEND), (3, 2, 0, SEND), (1, 2, 1), (1, 2, 1, SEND), (3, 2, 1, SEND),
+    (3, 1, 2), (3, 1, 1, SEND), (2, 1, 0, SEND), (0, 3, 2), (0, 3, 0, SEND), (1, 1, 2), (1, 1, 1, SEND),
+    (1, 1, 0, SEND), (1, 3, 1), (1, 3, 1, SEND), (0, 2, 2), (3, 3, 1), (0, 2, 0, SEND), (3, 3, 1, SEND),
+    (0, 1, 2), (3, 1, 0, SEND), (0, 2, 1, SEND), (0, 0, 2), (2, 0, 2), (2, 0, 1, SEND), (0, 1, 1, SEND),
+    (2, 0, 0, SEND), (3, 0, 2), (3, 0, 1, SEND), (1, 0, 2), (1, 0, 0, SEND), (0, 3, 1, SEND), (0, 1, 0, SEND),
+    (1, 0, 1, SEND), (3, 0, 0, SEND),
 )
 
 
@@ -105,11 +105,11 @@
     def greet(partner):
         pl.semaphore_signal(barrier, inc=1, device_id=partner, device_id_type=pl.DeviceIdType.MESH)
 
-    for partner in [row_at(sibling), *neighbours.values()]:
-        greet(partner)
     row_partners = [(2, has[2]), (-2, has[-2]), (beyond, has_beyond)]
     for by, condition in row_partners:
         where(condition, functools.partial(greet, row_at(by)))
+    for partner in [row_at(sibling), *neighbours.values()]:
+        greet(partner)
     expected = 1 + len(neighbours) + sum(condition.astype(jnp.int32) for _, condition in row_partners)
     loads = [
         pltpu.make_async_copy(src_ref, src, load_sem.at[1]),

time: 37.2 us -> 37.7 us (1.013)
  the two profiles are of different devices: /device:TPU:16 before, /device:TPU:66 now
where the time goes in v2:
time: 37.7 us; the launch traced here: 37.6 us
  Pallas kernels  36.2 us (96%)
  local copies, waits for them, and re-layouts  0.67 us (2%)
  between operations  0.66 us (2%)
    pallas_call x1, Pallas kernels, per_device(): pl.pallas_call(functools.partial(kernel, size, rows), out_shape=pltpu.VME...  36.2 us

profile of v2, /device:TPU:66, one launch (start us, length us, event | category | flops | bytes accessed | tf_op | source)
XLA Modules:
  0.0 37.6 jit_solution(3127488297566016120)
XLA Ops:
  0.7 36.2 %shard_map.55 = f32[1,160,256]{2,1,0:T(8,128)S(1)} custom-call(bf16[1,160,256]{2,1,0:T(8,128)(2,1)} %amp_ref.1, s32[1]{0:T(128)S(6)} %copy.8.edge_ref, s32[5,1,16]{2,1,0:T(1,128)} %bitcast.2, s32[1,16]{1,0:T(1,128)} %bitcast.3, bf16[16,1,5,160,160]{4,3,2,1,0:T(8,128)(2,1)} %weight_ref.1), custom_call_target="tpu_custom_call" | custom-call | flops 1048576000 | bytes 4096000 | tf_op jit(solution)/shard_map/pallas_call | solution.py:247
  36.9 0.7 %copy.7 = f32[1,160,256]{2,1,0:T(8,128)} copy(f32[1,160,256]{2,1,0:T(8,128)S(1)} %shard_map.55) | data formatting | bytes 327680
